TPU v7x, 32 devices: a whole 2x2x4 slice. The times are simulated.
32 devices in a mesh: ctx: 16 (over z, y, x), head: 2 (over core).
Axes of the slice: x: 2, y: 2, z: 4, core: 2. Of those that a mesh axis runs over, the one named last changes fastest.
Arguments:
- lin_query: bfloat16 [4096, 4096], P('ctx', 'head'), may hold values from -200 to 200
- lin_keys: bfloat16 [4096, 4096], P('ctx', 'head'), may hold values from -6 to 6
- lin_values: bfloat16 [4096, 4096], P('ctx', 'head'), may hold values from -6 to 6
- lin_grad: bfloat16 [4096, 4096], P('ctx', 'head'), may hold values from -6 to 6
- norm_gain: float32 [4096], P('head'), may hold values from 0.1 to 1.9
- log_decay: float32 [32, 4096], P('head'), may hold values from -1 to 0, as said below
- state_in: bfloat16 [16, 32, 128, 128], P('ctx', 'head'), may hold values from -96 to 96
- soft_query: bfloat16 [4096, 8192], P('ctx', 'head'), may hold values from -10 to 10
- soft_keys: bfloat16 [4096, 1024], P('ctx', 'head'), may hold values from -4 to 4
- soft_values: bfloat16 [4096, 1024], P('ctx', 'head'), may hold values from -6 to 6
- soft_grad: bfloat16 [4096, 8192], P('ctx', 'head'), may hold values from -6 to 6
- projections: bfloat16 [2, 4096, 1024], P(None, None, 'head'), may hold values from -0.125 to 0.125
- doc_lengths: int32 [8], replicated, may hold values from 1 to 768, 4096 in all
Outputs:
- lin_dq: bfloat16 [4096, 4096], P('ctx', 'head')
- lin_dk: bfloat16 [4096, 4096], P('ctx', 'head')
- lin_dv: bfloat16 [4096, 4096], P('ctx', 'head')
- soft_dq: bfloat16 [4096, 8192], P('ctx', 'head')
- soft_dk: bfloat16 [4096, 1024], P('ctx', 'head')
- soft_dv: bfloat16 [4096, 1024], P('ctx', 'head')
Inputs may be any that keep to these rules, and one draw needn't show every extreme that they name: `log_decay`: strictly negative. `doc_lengths`: positive lengths that add up to 4096; the largest is exactly 768.
All inputs are finite; a program needn't handle non-finite values.
Results may differ from a plain program's by a relative error of at most 0.011.
Values may be sent and summed in bfloat16 or wider, within the bound.
A program may use at most 128 MiB of HBM per device.

v0:
```python
import functools
import math

import jax
import jax.numpy as jnp
from jax import lax
from jax.experimental import pallas as pl
from jax.experimental.pallas import tpu as pltpu
from jax.sharding import PartitionSpec as P

DH = 128
Q_HEADS = 64
KV_HEADS = 8
LIGHTNING_HEADS = 32
SUB = 4
PAIR = 2

epsilon = 1e-06
precise = lax.Precision.HIGHEST
MESH = pl.DeviceIdType.MESH
LAST = (((1,), (1,)), ((), ()))
FIRST = (((0,), (0,)), ((), ()))
PLAIN = (((1,), (0,)), ((), ()))


def mm(a, b, dims):
    return lax.dot_general(a, b, dims, preferred_element_type=jnp.float32)


def signal(barrier, target):
    pl.semaphore_signal(barrier, inc=1, device_id=target, device_id_type=MESH)


def soft_kernel(
    chain, heads, q, g, k, v, qdoc, kdoc, proj,
    dq, dk, dv, kvg, projall,
    win, bias, acc, own, ret, back,
    win_send, win_recv, ret_send, ret_recv, kvg_send, kvg_recv, proj_send, proj_recv, proj_own,
):
    me = lax.axis_index("ctx")
    hd = lax.axis_index("head")
    L = q.shape[0]
    kvl = k.shape[1] // DH
    group = q.shape[1] // k.shape[1]
    half_rows = L // 2
    W = SUB * L - half_rows
    fl = projall.shape[2]
    own_at = (SUB - 1) * L

    barrier = pltpu.get_barrier_semaphore()
    for d in range(1, SUB):
        @pl.when(me + d < chain)
        def _():
            signal(barrier, {"ctx": me + d})

        @pl.when(me >= d)
        def _():
            signal(barrier, {"ctx": me - d})
    for j in range(1, heads):
        signal(barrier, {"head": lax.rem(hd + j, heads)})
    for c in range(kvl):
        win[0, c, own_at:, :] = k[:, c * DH : (c + 1) * DH]
        win[1, c, own_at:, :] = v[:, c * DH : (c + 1) * DH]
    pl.semaphore_wait(
        barrier, jnp.minimum(me, SUB - 1) + jnp.minimum(chain - 1 - me, SUB - 1) + (heads - 1)
    )

    def window_copy(d, c):
        return pltpu.make_async_remote_copy(
            src_ref=win.at[:, c, pl.ds(own_at, L), :],
            dst_ref=win.at[:, c, pl.ds((SUB - 1 - d) * L, L), :],
            send_sem=win_send.at[d - 1, c],
            recv_sem=win_recv.at[d - 1, c],
            device_id={"ctx": me + d},
            device_id_type=MESH,
        )

    def return_copy(d, c):
        return pltpu.make_async_remote_copy(
            src_ref=ret.at[d - 1, c],
            dst_ref=back.at[d - 1, c],
            send_sem=ret_send.at[d - 1, c],
            recv_sem=ret_recv.at[d - 1, c],
            device_id={"ctx": me - d},
            device_id_type=MESH,
        )

    def proj_copy(j):
        peer = lax.rem(hd + j, heads)
        return pltpu.make_async_remote_copy(
            src_ref=proj.at[:, pl.ds(peer * fl, fl), :],
            dst_ref=projall.at[hd],
            send_sem=proj_send.at[j - 1],
            recv_sem=proj_recv.at[j - 1],
            device_id={"head": peer},
            device_id_type=MESH,
        )

    def kvg_copy(j):
        return pltpu.make_async_remote_copy(
            src_ref=kvg.at[hd],
            dst_ref=kvg.at[hd],
            send_sem=kvg_send.at[j - 1],
            recv_sem=kvg_recv.at[j - 1],
            device_id={"head": lax.rem(hd + j, heads)},
            device_id_type=MESH,
        )

    for c in range(kvl):
        for d in range(1, SUB):
            @pl.when(me + d < chain)
            def _(d=d, c=c):
                window_copy(d, c).start()
    own_proj = pltpu.make_async_copy(proj.at[:, pl.ds(hd * fl, fl), :], projall.at[hd], proj_own)
    own_proj.start()
    for j in range(1, heads):
        proj_copy(j).start()

    for d in range(1, SUB):
        @pl.when(me < d)
        def _(d=d):
            at = (SUB - 1 - d) * L
            win[:, :, at : at + L, :] = jnp.zeros((2, kvl, L, DH), win.dtype)

    for half in range(2):
        r = half * half_rows
        later = lax.broadcasted_iota(jnp.int32, (W, half_rows), 0) - own_at
        row = lax.broadcasted_iota(jnp.int32, (W, half_rows), 1)
        same = kdoc[r : r + W, :] == qdoc[:, r : r + half_rows]
        bias[half] = jnp.where(same & (later <= row), 0.0, -1e30)

    score_scale = DH ** (-0.5)
    to_base2 = score_scale * math.log2(math.e)

    def kv_turn(c, carry):
        for d in range(1, SUB):
            @pl.when(me >= d)
            def _(d=d):
                window_copy(d, c).wait_recv()
        acc[...] = jnp.zeros(acc.shape, acc.dtype)

        def turn(i, inner):
            half = i // (group // PAIR)
            pair = i % (group // PAIR)
            r = pl.multiple_of(half * half_rows, half_rows)
            rows = pl.ds(r, half_rows)
            col = pl.multiple_of((c * group + pair * PAIR) * DH, DH)
            cols = pl.ds(col, PAIR * DH)
            q_wide = q[rows, cols]
            g_wide = g[rows, cols]
            q_rows = jnp.concatenate([q_wide[:, x * DH : (x + 1) * DH] for x in range(PAIR)], 0)
            g_rows = jnp.concatenate([g_wide[:, x * DH : (x + 1) * DH] for x in range(PAIR)], 0)
            k_win = win[0, c, pl.ds(r, W), :]
            v_win = win[1, c, pl.ds(r, W), :]
            b = bias[half]
            s = mm(k_win, q_rows, LAST) * to_base2 + jnp.concatenate([b] * PAIR, 1)
            m = jnp.max(s, axis=0, keepdims=True)
            e = jnp.exp2(s - m)
            total = jnp.sum(e, axis=0, keepdims=True)
            dp = mm(v_win, g_rows, LAST)
            inv = 1.0 / total
            delta = jnp.sum(e * dp, axis=0, keepdims=True) * inv
            p = e * inv
            p_low = p.astype(jnp.bfloat16)
            ds = (p * (dp - delta)).astype(jnp.bfloat16)
            acc[0, pl.ds(r, W), :] += mm(ds, q_rows, PLAIN)
            acc[1, pl.ds(r, W), :] += mm(p_low, g_rows, PLAIN)
            dq_t = mm(k_win, ds, FIRST) * score_scale
            dq_rows = dq_t.T.astype(jnp.bfloat16)
            dq[rows, cols] = jnp.concatenate(
                [dq_rows[x * half_rows : (x + 1) * half_rows] for x in range(PAIR)], 1
            )
            return inner

        lax.fori_loop(0, 2 * (group // PAIR), turn, 0)
        own[0, c] = acc[0, own_at:, :] * score_scale
        own[1, c] = acc[1, own_at:, :]
        for d in range(1, SUB):
            at = (SUB - 1 - d) * L

            @pl.when(me >= d)
            def _(d=d, at=at):
                ret[d - 1, c, 0] = (acc[0, at : at + L, :] * score_scale).astype(ret.dtype)
                ret[d - 1, c, 1] = acc[1, at : at + L, :].astype(ret.dtype)
                return_copy(d, c).start()
        return carry

    lax.fori_loop(0, kvl, kv_turn, 0)

    for c in range(kvl):
        for d in range(1, SUB):
            @pl.when(me + d < chain)
            def _(d=d, c=c):
                return_copy(d, c).wait_recv()
                own[:, c] = own[:, c] + back[d - 1, c].astype(jnp.float32)
        low = own[:, c].astype(jnp.bfloat16)
        kvg[hd, 0, :, c * DH : (c + 1) * DH] = low[0]
        kvg[hd, 1, :, c * DH : (c + 1) * DH] = low[1]
        dk[:, c * DH : (c + 1) * DH] = low[0]
        dv[:, c * DH : (c + 1) * DH] = low[1]
    for j in range(1, heads):
        kvg_copy(j).start()

    for c in range(kvl):
        for d in range(1, SUB):
            @pl.when(me + d < chain)
            def _(d=d, c=c):
                window_copy(d, c).wait_send()

            @pl.when(me >= d)
            def _(d=d, c=c):
                return_copy(d, c).wait_send()
    own_proj.wait()
    for j in range(1, heads):
        proj_copy(j).wait()
    for j in range(1, heads):
        kvg_copy(j).wait()


def document_of(positions, doc_lengths):
    doc_ends = jnp.cumsum(doc_lengths)
    return jnp.sum((doc_ends[None, :] <= positions[:, None]).astype(jnp.int32), axis=1)


def softmax_part(soft_query, soft_keys, soft_values, soft_grad, projections, doc_lengths):
    L = soft_query.shape[0]
    chain = lax.axis_size("ctx")
    heads = lax.axis_size("head")
    kvl = soft_keys.shape[1] // DH
    fl = projections.shape[1] // heads
    first = lax.axis_index("ctx") * L
    query_pos = first + jnp.arange(L, dtype=jnp.int32)
    key_pos = first - (SUB - 1) * L + jnp.arange(SUB * L, dtype=jnp.int32)
    qdoc = document_of(query_pos, doc_lengths)[None, :]
    kdoc = jnp.where(key_pos >= 0, document_of(key_pos, doc_lengths), -1)[:, None]
    half_rows = L // 2
    W = SUB * L - half_rows
    vm = pl.BlockSpec(memory_space=pltpu.VMEM)
    anywhere = pl.BlockSpec(memory_space=pl.ANY)
    bf, f32 = jnp.bfloat16, jnp.float32
    sem = pltpu.SemaphoreType.DMA
    kv_cols = soft_keys.shape[1]
    return pl.pallas_call(
        functools.partial(soft_kernel, chain, heads),
        out_shape=(
            jax.ShapeDtypeStruct(soft_query.shape, bf),
            jax.ShapeDtypeStruct(soft_keys.shape, bf),
            jax.ShapeDtypeStruct(soft_keys.shape, bf),
            jax.ShapeDtypeStruct((heads, 2, L, kv_cols), bf),
            jax.ShapeDtypeStruct((heads, 2, fl, kv_cols), bf),
        ),
        in_specs=[vm] * 6 + [anywhere],
        out_specs=(vm, vm, vm, vm, anywhere),
        scratch_shapes=[
            pltpu.VMEM((2, kvl, SUB * L, DH), bf),
            pltpu.VMEM((2, W, half_rows), f32),
            pltpu.VMEM((2, SUB * L, DH), f32),
            pltpu.VMEM((2, kvl, L, DH), f32),
            pltpu.VMEM((SUB - 1, kvl, 2, L, DH), bf),
            pltpu.VMEM((SUB - 1, kvl, 2, L, DH), bf),
            sem((SUB - 1, kvl)),
            sem((SUB - 1, kvl)),
            sem((SUB - 1, kvl)),
            sem((SUB - 1, kvl)),
            sem((max(1, heads - 1),)),
            sem((max(1, heads - 1),)),
            sem((max(1, heads - 1),)),
            sem((max(1, heads - 1),)),
            sem,
        ],
        compiler_params=pltpu.CompilerParams(
            collective_id=0, has_side_effects=True, vmem_limit_bytes=56 * 1024 * 1024
        ),
        name="softmax_layer",
    )(soft_query, soft_grad, soft_keys, soft_values, qdoc, kdoc, projections)


def decay_weights(log_block):
    running = jnp.cumsum(log_block, axis=1)
    position = jnp.arange(log_block.shape[1], dtype=jnp.int32)
    before = position[:, None] >= position[None, :]
    log_gap = running[:, :, None] - running[:, None, :]
    weights = jnp.where(before[None], jnp.exp(jnp.minimum(log_gap, 0.0)), 0.0)
    return (running, weights)


def lightning_part(lin_query, lin_keys, lin_values, cotangent, norm_gain, log_decay, state_in):
    length = lin_query.shape[0]
    head_count = lin_query.shape[1] // DH
    device = lax.axis_index("ctx")
    chain = lax.axis_size("ctx")
    log_block = lax.dynamic_slice_in_dim(log_decay, device * length, length, 1)
    running, weights = decay_weights(log_block)
    query_blk = lin_query.reshape(length, head_count, DH)
    key_blk = lin_keys.reshape(length, head_count, DH)
    value_blk = lin_values.reshape(length, head_count, DH)
    grad_blk = cotangent.reshape(length, head_count, DH)
    state_blk = state_in[0]
    near_terms = (
        jnp.einsum("thd,shd->hts", query_blk, key_blk, preferred_element_type=jnp.float32) * weights
    ).astype(jnp.bfloat16)
    growth = jnp.exp(running).T[:, :, None]
    scaled = (query_blk.astype(jnp.float32) * growth).astype(jnp.bfloat16)
    inside = jnp.einsum("hts,shd->thd", near_terms, value_blk, preferred_element_type=jnp.float32)
    carried = jnp.einsum("thd,hde->the", scaled, state_blk, preferred_element_type=jnp.float32)
    lin_out = (inside + carried) / DH
    gated = norm_gain.reshape(head_count, DH)[None] * grad_blk
    squares, cross_term = lax.psum(
        (jnp.sum(lin_out * lin_out, axis=(1, 2)), jnp.sum(gated * lin_out, axis=(1, 2))), "head"
    )
    features = LIGHTNING_HEADS * DH
    spread = jnp.sqrt(squares / features + epsilon)
    out_grad = (
        gated / spread[:, None, None]
        - lin_out * (cross_term / (features * spread**3))[:, None, None]
    ).astype(jnp.bfloat16)
    far_terms = (
        jnp.einsum("the,she->hts", out_grad, value_blk, preferred_element_type=jnp.float32)
        * weights
    ).astype(jnp.bfloat16)
    grad_query = (
        jnp.einsum("hts,shd->thd", far_terms, key_blk, preferred_element_type=jnp.float32)
        + growth
        * jnp.einsum("the,hde->thd", out_grad, state_blk, preferred_element_type=jnp.float32)
    ) / DH
    summary = jnp.einsum(
        "thd,the->hde", scaled, out_grad, preferred_element_type=jnp.float32
    ).astype(jnp.bfloat16)
    own_total = running[:, -1]
    totals = jnp.sum(log_decay.reshape(head_count, chain, length), axis=2)
    starts = jnp.concatenate(
        [jnp.zeros((head_count, 1), jnp.float32), jnp.cumsum(totals, axis=1)], axis=1
    )
    anchor = lax.dynamic_slice_in_dim(starts, device + 1, 1, 1)
    block_in = lax.all_gather(summary[None], "ctx", axis=0, tiled=True)
    block_count = block_in.shape[0]
    block_index = jnp.arange(block_count, dtype=jnp.int32)
    log_level = lax.slice_in_dim(starts, 0, block_count, axis=1)
    factors = jnp.where(
        block_index[None, :] > device, jnp.exp(jnp.minimum(log_level - anchor, 0.0)), 0.0
    )
    after_state = jnp.einsum(
        "hn,nhde->hde", factors, block_in.astype(jnp.float32), precision=precise
    )
    after_low = after_state.astype(jnp.bfloat16)
    tail_decay = jnp.exp(own_total[:, None] - running).T[:, :, None]
    grad_key = (
        jnp.einsum("hst,shd->thd", far_terms, query_blk, preferred_element_type=jnp.float32)
        + tail_decay
        * jnp.einsum("the,hde->thd", value_blk, after_low, preferred_element_type=jnp.float32)
    ) / DH
    grad_value = (
        jnp.einsum("hst,she->the", near_terms, out_grad, preferred_element_type=jnp.float32)
        + tail_decay
        * jnp.einsum("thd,hde->the", key_blk, after_low, preferred_element_type=jnp.float32)
    ) / DH
    flat = (length, head_count * DH)
    return (
        grad_query.astype(jnp.bfloat16).reshape(flat),
        grad_key.astype(jnp.bfloat16).reshape(flat),
        grad_value.astype(jnp.bfloat16).reshape(flat),
    )


def per_device(
    lin_query,
    lin_keys,
    lin_values,
    lin_grad,
    norm_gain,
    log_decay,
    state_in,
    soft_query,
    soft_keys,
    soft_values,
    soft_grad,
    projections,
    doc_lengths,
):
    soft_dq, soft_dk, soft_dv, kv_grads, projected = softmax_part(
        soft_query, soft_keys, soft_values, soft_grad, projections, doc_lengths
    )
    carried_back = jnp.einsum(
        "hctk,hcfk->tf", kv_grads, projected, preferred_element_type=jnp.float32
    )
    cotangent = lin_grad.astype(jnp.float32) + carried_back
    lin_dq, lin_dk, lin_dv = lightning_part(
        lin_query, lin_keys, lin_values, cotangent, norm_gain, log_decay, state_in
    )
    return (lin_dq, lin_dk, lin_dv, soft_dq, soft_dk, soft_dv)


def solution(mesh):
    in_specs = (
        P("ctx", "head"),
        P("ctx", "head"),
        P("ctx", "head"),
        P("ctx", "head"),
        P("head"),
        P("head", None),
        P("ctx", "head", None, None),
        P("ctx", "head"),
        P("ctx", "head"),
        P("ctx", "head"),
        P("ctx", "head"),
        P(None, None, "head"),
        P(),
    )
    out_specs = (
        P("ctx", "head"),
        P("ctx", "head"),
        P("ctx", "head"),
        P("ctx", "head"),
        P("ctx", "head"),
        P("ctx", "head"),
    )
    return jax.shard_map(
        per_device, mesh=mesh, in_specs=in_specs, out_specs=out_specs, check_vma=False
    )
```

profile of v0, /device:TPU:24, one launch (start us, length us, event | category | flops | bytes accessed | tf_op | source)
XLA Modules:
  0.0 319.5 jit_solution(1994324928256667841)
XLA Ops:
  7.3 0.8 copy_bitcast_fusion.1
  8.1 0.6 reduce-window.19
  8.6 0.2 slice_reduce_fusion
  8.9 0.2 slice_reduce_fusion.1
  9.1 0.1 exponential_bitcast_fusion
  9.2 0.8 reduce-window.18
  10.1 0.1 convert_reduce_fusion
  10.1 0.2 copy.112
  10.4 0.9 fusion.39.kdoc
  11.2 0.6 convert_reduce_fusion.1
  11.9 135.6 %softmax_layer.1 = (bf16[256,4096]{1,0:T(8,128)(2,1)}, bf16[256,512]{1,0:T(8,128)(2,1)}, bf16[256,512]{1,0:T(8,128)(2,1)}, bf16[2,2,256,512]{3,2,1,0:T(8,128)(2,1)}, bf16[2,2,2048,512]{3,2,1,0:T(8,128)(2,1)}) custom-call(bf16[256,4096]{1,0:T(8,128)(2,1)} %q.1, bf16[256,4096]{1,0:T(8,128)(2,1)} %g.1, bf16[256,512]{1,0:T(8,128)(2,1)} %k.1, ...), custom_call_target="tpu_custom_call" | custom-call | tf_op jit(solution)/shard_map/softmax_layer/pallas_call | solution.py:243
  147.5 7.4 %fusion.7 = f32[256,2048]{1,0:T(8,128)} fusion(bf16[2,2,2048,512]{3,2,1,0:T(8,128)(2,1)} %get-tuple-element.12, bf16[256,2048]{1,0:T(8,128)(2,1)S(1)} %copy-done.18, bf16[2,2,256,512]{3,2,1,0:T(8,128)(2,1)} %get-tuple-element.11), kind=kOutput, calls=%fused_computation.8 | convolution fusion | flops 2148532224 | bytes 12582912 | tf_op jit(solution)/shard_map/hctk,hcfk->tf/dot_general | solution.py:383
  154.8 1.9 copy.146
  156.8 2.3 copy.116
  159.0 2.7 multiply_convert_fusion.1
  161.8 0.8 fusion.22
  162.7 0.5 copy-done.6
  163.2 0.6 copy-done.1
  163.8 0.1 copy-done.11
  163.9 2.3 fusion.20
  166.2 2.6 all-reduce.1
  168.9 2.1 fusion.19
  170.9 1.0 copy-done.4
  171.9 1.3 convolution_convert_fusion
  173.2 0.1 copy.151
  173.3 0.1 reduce_sum.52
  173.4 0.2 reduce_window_sum.44
  173.6 2.6 multiply_convert_fusion
  176.3 0.8 fusion.26
  177.1 0.5 copy-done.7
  177.6 0.7 copy-done.5
  178.2 0.1 copy-done.12
  178.4 0.4 fusion.18
  178.8 1.4 copy.132
  180.2 0.2 dynamic-slice_reduce_fusion
  180.4 0.1 exponential_select_fusion.1
  180.5 3.6 %fusion.43 = f32[16,128,256]{2,1,0:T(8,128)} fusion(bf16[256,16,128]{0,2,1:T(8,128)(2,1)S(1)} %copy-done.5, bf16[16,256,256]{2,1,0:T(8,128)(2,1)} %copy-done.6), kind=kOutput, calls=%fused_computation.71 | convolution fusion | flops 268435456 | bytes 5242880 | tf_op jit(solution)/shard_map/hst,she->the/dot_general | solution.py:353
  184.1 0.4 fusion.44
  184.6 98.8 %all-gather.3.cloned.1.call-done = bf16[256,128,128]{2,1,0:T(8,128)(2,1)} async-done(((bf16[16,128,128]{2,1,0:T(8,128)(2,1)}), bf16[256,128,128]{2,1,0:T(8,128)(2,1)}) %all-gather.3.cloned.1.call-update) | async-done | bytes 8388624 | tf_op jit(solution)/shard_map/all_gather | solution.py:335
  283.4 12.3 %fusion = bf16[16,1,128,128]{3,1,2,0:T(2,128)(2,1)} fusion(f32[16,16,1,1]{1,2,3,0:T(1,128)S(1)} %bitcast.150, bf16[16,16,128,128]{3,2,1,0:T(8,128)(2,1)} %bitcast.139), kind=kOutput, calls=%fused_computation | convolution fusion | flops 50331648 | bytes 8913920 | tf_op jit(solution)/shard_map/hn,nhde->hde/dot_general | solution.py:342
  295.7 3.5 %copy.144 = bf16[16,1,128,128]{2,3,0,1:T(8,128)(2,1)} copy(bf16[16,1,128,128]{3,1,2,0:T(2,128)(2,1)} %fusion) | data formatting | bytes 1048576 | tf_op jit(solution)/shard_map/hn,nhde->hde/dot_general | solution.py:342
  299.1 3.2 fusion.12
  302.3 2.3 copy.134
  304.6 2.9 fusion.15
  307.5 2.4 copy.133
  309.9 1.3 copy.195
  311.2 0.7 copy.196
  311.9 0.7 copy.197
  (41 shorter events, 0.3 us)
Async XLA Ops:
  7.2 151.9 %copy-start = (bf16[256,2048]{1,0:T(8,128)(2,1)S(1)}, bf16[256,2048]{1,0:T(8,128)(2,1)}, u32[]{:S(2)}) copy-start(bf16[256,2048]{1,0:T(8,128)(2,1)} %param.14) | copy-start | bytes 3145732
  7.2 276.2 %all-gather.3.cloned.1.call-start = ((), (), s32[]{:S(2)}) async-start(), calls=%async_computation | async-start | bytes 8912896 | tf_op jit(solution)/shard_map/all_gather | solution.py:335
  11.9 135.6 %copy-start.18 = (bf16[256,2048]{1,0:T(8,128)(2,1)S(1)}, bf16[256,2048]{1,0:T(8,128)(2,1)}, u32[]{:S(2)}) copy-start(bf16[256,2048]{1,0:T(8,128)(2,1)} %param.16) | copy-start | bytes 3145732
  159.0 2.7 copy-start.9
  161.8 1.4 copy-start.6
  161.8 2.0 copy-start.1
  161.8 2.1 copy-start.11
  161.8 2.1 copy-start.17
  168.9 3.0 copy-start.2
  170.9 1.0 copy-start.4
  171.9 1.3 copy-start.14
  171.9 1.7 copy-start.10
  176.2 1.3 copy-start.7
  176.2 2.0 copy-start.5
  176.3 2.1 copy-start.12
  180.5 3.6 %copy-start.3 = (bf16[256,2048]{0,1:T(8,128)(2,1)S(1)}, bf16[256,2048]{0,1:T(8,128)(2,1)}, u32[]{:S(2)}) copy-start(bf16[256,2048]{0,1:T(8,128)(2,1)} %copy.116) | copy-start | bytes 3145732
  180.5 3.6 %copy-start.8 = (bf16[16,256,256]{2,1,0:T(8,128)(2,1)S(1)}, bf16[16,256,256]{2,1,0:T(8,128)(2,1)}, u32[]{:S(2)}) copy-start(bf16[16,256,256]{2,1,0:T(8,128)(2,1)} %copy-done.7) | copy-start | bytes 6291460
  307.5 2.4 copy-start.13
  309.9 1.3 copy-start.16
  309.9 2.0 copy-start.15
Sparse Core Ops, SparseCore 0:
  173.3 110.0 all-gather.2
where the time goes:
time: 324 us; the launch traced here: 319 us
  Pallas kernels  136 us (42%)
  waiting for transfers between devices  98.8 us (30%)
  matrix products  40.8 us (13%)
  local copies, waits for them, and re-layouts  21.7 us (7%)
  between operations  14.3 us (4%)
  other arithmetic  5.67 us (2%)
    pallas_call x1, Pallas kernels, softmax_part(): pl.pallas_call(functools.partial(soft_kernel, chain, heads), out_shape=(j...  136 us
    all_gather x1, waiting for transfers between devices, lightning_part(): block_in = lax.all_gather(summary[None], 'ctx', axis=0, tiled=True)  98.8 us
    unnamed x46, local copies, waits for them, and re-layouts  14.7 us
    dot_general x1, matrix products, lightning_part(): jnp.einsum('hn,nhde->hde', factors, block_in.astype(jnp.float32), precisi...  12.3 us
    dot_general x1, matrix products, per_device(): jnp.einsum('hctk,hcfk->tf', kv_grads, projected, preferred_element_type=j...  7.4 us
  transfers between devices with their start and end apart: 1, of which 1 were waited for; matrix products, arithmetic and copies ran while one was open for 3% of the time, Pallas kernels for 0%

commit v1 on v0

--- a/solution.py
+++ b/solution.py
@@ -16,7 +16,6 @@
 PAIR = 2
 
 epsilon = 1e-06
-precise = lax.Precision.HIGHEST
 MESH = pl.DeviceIdType.MESH
 LAST = (((1,), (1,)), ((), ()))
 FIRST = (((0,), (0,)), ((), ()))
@@ -275,91 +274,203 @@
     )(soft_query, soft_grad, soft_keys, soft_values, qdoc, kdoc, projections)
 
 
-def decay_weights(log_block):
+def masked_decay(col, row):
+    L = col.shape[0]
+    at = lax.broadcasted_iota(jnp.int32, (L, L), 0)
+    earlier = lax.broadcasted_iota(jnp.int32, (L, L), 1) <= at
+    return jnp.where(earlier, jnp.exp(jnp.where(earlier, col - row, 0.0)), 0.0)
+
+
+def forward_kernel(q, k, v, lg, gain, row, col, state, kvg, proj, out, gated, near, squares, cross):
+    weights = masked_decay(col[0], row[0])
+    near_low = (mm(q[...], k[...], LAST) * weights).astype(jnp.bfloat16)
+    near[0] = near_low
+    scaled = (q[...].astype(jnp.float32) * jnp.exp(col[0])).astype(jnp.bfloat16)
+    lin_out = (mm(near_low, v[...], PLAIN) + mm(scaled, state[0, 0], PLAIN)) / DH
+    cotangent = lg[...].astype(jnp.float32)
+    for x in range(kvg.shape[0]):
+        for y in range(2):
+            cotangent = cotangent + mm(kvg[x, y], proj[x, y], LAST)
+    gated_now = gain[...] * cotangent
+    out[...] = lin_out
+    gated[...] = gated_now
+
+    @pl.when(pl.program_id(0) == 0)
+    def _():
+        squares[...] = jnp.zeros_like(squares)
+        cross[...] = jnp.zeros_like(cross)
+
+    squares[...] += jnp.sum(lin_out * lin_out, axis=1, keepdims=True)
+    cross[...] += jnp.sum(gated_now * lin_out, axis=1, keepdims=True)
+
+
+def norm_kernel(out, gated, squares, cross, q, col, dout, summary):
+    features = LIGHTNING_HEADS * DH
+    spread = jnp.sqrt(squares[...] / features + epsilon)
+    low = (
+        gated[...] / spread - out[...] * (cross[...] / (features * spread * spread * spread))
+    ).astype(jnp.bfloat16)
+    dout[...] = low
+    scaled = (q[...].astype(jnp.float32) * jnp.exp(col[0])).astype(jnp.bfloat16)
+    summary[0] = mm(scaled, low, FIRST).astype(jnp.bfloat16)
+
+
+def inner_kernel(q, k, v, dout, near, state, row, col, dq, part_key, part_value):
+    weights = masked_decay(col[0], row[0])
+    far = (mm(dout[...], v[...], LAST) * weights).astype(jnp.bfloat16)
+    carried = mm(dout[...], state[0, 0], LAST)
+    dq[...] = ((mm(far, k[...], PLAIN) + jnp.exp(col[0]) * carried) / DH).astype(jnp.bfloat16)
+    part_key[...] = mm(far, q[...], FIRST)
+    part_value[...] = mm(near[0], dout[...], FIRST)
+
+
+def outer_kernel(k, v, part_key, part_value, col, after, dk, dv):
+    running = col[0]
+    tail = jnp.exp(running[running.shape[0] - 1 :, :] - running)
+    dk[...] = ((part_key[...] + tail * mm(v[...], after[0], LAST)) / DH).astype(jnp.bfloat16)
+    dv[...] = ((part_value[...] + tail * mm(k[...], after[0], PLAIN)) / DH).astype(jnp.bfloat16)
+
+
+PLANE = 4
+
+
+def later_states(summary, starts):
+    chain = lax.axis_size("ctx")
+    groups = chain // PLANE
+    me = lax.axis_index("ctx")
+    z, j = me // PLANE, me % PLANE
+    part = summary.shape[0] // PLANE
+
+    def within(block, d):
+        route = [(i, i // PLANE * PLANE + (i + d) % PLANE) for i in range(chain)]
+        return lax.ppermute(block, "ctx", route)
+
+    def quarter(array, at):
+        return lax.dynamic_slice_in_dim(array, at * part, part, 0)
+
+    pieces = [quarter(summary, j)]
+    for d in range(1, PLANE):
+        pieces.append(within(quarter(summary, (j + d) % PLANE), d))
+    pieces = [piece.astype(jnp.float32) for piece in pieces]
+    levels = quarter(starts, j)
+    local = lax.dynamic_slice_in_dim(levels, z * PLANE, PLANE + 1, 1)
+    source = (j - jnp.arange(PLANE)) % PLANE
+    target = (j + jnp.arange(PLANE)) % PLANE
+    from_level = jnp.take(local, source, axis=1)
+    to_level = jnp.take(local, target + 1, axis=1)
+    to_first = jnp.exp(jnp.minimum(from_level - local[:, :1], 0.0))
+    factors = jnp.where(
+        source[None, :, None] > target[None, None, :],
+        jnp.exp(jnp.minimum(from_level[:, :, None] - to_level[:, None, :], 0.0)),
+        0.0,
+    )
+    whole = sum(to_first[:, d, None, None] * pieces[d] for d in range(PLANE))
+    whole = whole.astype(jnp.bfloat16)
+    carry = jnp.zeros(whole.shape, jnp.float32)
+    for e in range(1, groups):
+        arrived = lax.ppermute(
+            whole, "ctx", [(i, i - PLANE * e) for i in range(PLANE * e, chain)]
+        )
+        level = lax.dynamic_slice_in_dim(levels, jnp.minimum((z + e) * PLANE, chain), 1, 1)
+        decay = jnp.exp(jnp.minimum(level - local[:, PLANE:], 0.0))
+        carry = carry + decay[:, :, None] * arrived.astype(jnp.float32)
+    last = jnp.exp(jnp.minimum(local[:, PLANE:] - to_level, 0.0))
+    result = jnp.zeros(summary.shape, jnp.bfloat16)
+    for d in range(PLANE):
+        block = last[:, d, None, None] * carry
+        for x in range(PLANE):
+            block = block + factors[:, x, d, None, None] * pieces[x]
+        block = block.astype(jnp.bfloat16)
+        if d:
+            block = within(block, d)
+        result = lax.dynamic_update_slice_in_dim(result, block, (j - d) % PLANE * part, 0)
+    return result
+
+
+def lightning_part(
+    lin_query, lin_keys, lin_values, lin_grad, norm_gain, log_decay, state_in, kv_grads, projected
+):
+    L, width = lin_query.shape
+    hl = width // DH
+    chain = lax.axis_size("ctx")
+    log_block = lax.dynamic_slice_in_dim(log_decay, lax.axis_index("ctx") * L, L, 1)
     running = jnp.cumsum(log_block, axis=1)
-    position = jnp.arange(log_block.shape[1], dtype=jnp.int32)
-    before = position[:, None] >= position[None, :]
-    log_gap = running[:, :, None] - running[:, None, :]
-    weights = jnp.where(before[None], jnp.exp(jnp.minimum(log_gap, 0.0)), 0.0)
-    return (running, weights)
-
-
-def lightning_part(lin_query, lin_keys, lin_values, cotangent, norm_gain, log_decay, state_in):
-    length = lin_query.shape[0]
-    head_count = lin_query.shape[1] // DH
-    device = lax.axis_index("ctx")
-    chain = lax.axis_size("ctx")
-    log_block = lax.dynamic_slice_in_dim(log_decay, device * length, length, 1)
-    running, weights = decay_weights(log_block)
-    query_blk = lin_query.reshape(length, head_count, DH)
-    key_blk = lin_keys.reshape(length, head_count, DH)
-    value_blk = lin_values.reshape(length, head_count, DH)
-    grad_blk = cotangent.reshape(length, head_count, DH)
-    state_blk = state_in[0]
-    near_terms = (
-        jnp.einsum("thd,shd->hts", query_blk, key_blk, preferred_element_type=jnp.float32) * weights
-    ).astype(jnp.bfloat16)
-    growth = jnp.exp(running).T[:, :, None]
-    scaled = (query_blk.astype(jnp.float32) * growth).astype(jnp.bfloat16)
-    inside = jnp.einsum("hts,shd->thd", near_terms, value_blk, preferred_element_type=jnp.float32)
-    carried = jnp.einsum("thd,hde->the", scaled, state_blk, preferred_element_type=jnp.float32)
-    lin_out = (inside + carried) / DH
-    gated = norm_gain.reshape(head_count, DH)[None] * grad_blk
-    squares, cross_term = lax.psum(
-        (jnp.sum(lin_out * lin_out, axis=(1, 2)), jnp.sum(gated * lin_out, axis=(1, 2))), "head"
-    )
-    features = LIGHTNING_HEADS * DH
-    spread = jnp.sqrt(squares / features + epsilon)
-    out_grad = (
-        gated / spread[:, None, None]
-        - lin_out * (cross_term / (features * spread**3))[:, None, None]
-    ).astype(jnp.bfloat16)
-    far_terms = (
-        jnp.einsum("the,she->hts", out_grad, value_blk, preferred_element_type=jnp.float32)
-        * weights
-    ).astype(jnp.bfloat16)
-    grad_query = (
-        jnp.einsum("hts,shd->thd", far_terms, key_blk, preferred_element_type=jnp.float32)
-        + growth
-        * jnp.einsum("the,hde->thd", out_grad, state_blk, preferred_element_type=jnp.float32)
-    ) / DH
-    summary = jnp.einsum(
-        "thd,the->hde", scaled, out_grad, preferred_element_type=jnp.float32
-    ).astype(jnp.bfloat16)
-    own_total = running[:, -1]
-    totals = jnp.sum(log_decay.reshape(head_count, chain, length), axis=2)
+    row, col = running[:, None, :], running[:, :, None]
+    totals = jnp.sum(log_decay.reshape(hl, chain, L), axis=2)
     starts = jnp.concatenate(
-        [jnp.zeros((head_count, 1), jnp.float32), jnp.cumsum(totals, axis=1)], axis=1
-    )
-    anchor = lax.dynamic_slice_in_dim(starts, device + 1, 1, 1)
-    block_in = lax.all_gather(summary[None], "ctx", axis=0, tiled=True)
-    block_count = block_in.shape[0]
-    block_index = jnp.arange(block_count, dtype=jnp.int32)
-    log_level = lax.slice_in_dim(starts, 0, block_count, axis=1)
-    factors = jnp.where(
-        block_index[None, :] > device, jnp.exp(jnp.minimum(log_level - anchor, 0.0)), 0.0
-    )
-    after_state = jnp.einsum(
-        "hn,nhde->hde", factors, block_in.astype(jnp.float32), precision=precise
-    )
-    after_low = after_state.astype(jnp.bfloat16)
-    tail_decay = jnp.exp(own_total[:, None] - running).T[:, :, None]
-    grad_key = (
-        jnp.einsum("hst,shd->thd", far_terms, query_blk, preferred_element_type=jnp.float32)
-        + tail_decay
-        * jnp.einsum("the,hde->thd", value_blk, after_low, preferred_element_type=jnp.float32)
-    ) / DH
-    grad_value = (
-        jnp.einsum("hst,she->the", near_terms, out_grad, preferred_element_type=jnp.float32)
-        + tail_decay
-        * jnp.einsum("thd,hde->the", key_blk, after_low, preferred_element_type=jnp.float32)
-    ) / DH
-    flat = (length, head_count * DH)
-    return (
-        grad_query.astype(jnp.bfloat16).reshape(flat),
-        grad_key.astype(jnp.bfloat16).reshape(flat),
-        grad_value.astype(jnp.bfloat16).reshape(flat),
-    )
+        [jnp.zeros((hl, 1), jnp.float32), jnp.cumsum(totals, axis=1)], axis=1
+    )
+    bf, f32 = jnp.bfloat16, jnp.float32
+    H, _, _, kc = kv_grads.shape
+    wide = pl.BlockSpec((L, DH), lambda h: (0, h))
+    row_spec = pl.BlockSpec((1, 1, L), lambda h: (h, 0, 0))
+    col_spec = pl.BlockSpec((1, L, 1), lambda h: (h, 0, 0))
+    state_spec = pl.BlockSpec((1, 1, DH, DH), lambda h: (0, h, 0, 0))
+    square_spec = pl.BlockSpec((1, L, L), lambda h: (h, 0, 0))
+    matrix_spec = pl.BlockSpec((1, DH, DH), lambda h: (h, 0, 0))
+    sum_spec = pl.BlockSpec((L, 1), lambda h: (0, 0))
+    shape = jax.ShapeDtypeStruct
+
+    def call(body, name, ins, outs, flops, *args):
+        return pl.pallas_call(
+            body,
+            grid=(hl,),
+            in_specs=ins,
+            out_specs=tuple(spec for spec, _ in outs),
+            out_shape=tuple(kind for _, kind in outs),
+            cost_estimate=pl.CostEstimate(
+                flops=flops * hl, bytes_accessed=hl * L * DH * 16, transcendentals=hl * L * L
+            ),
+            compiler_params=pltpu.CompilerParams(vmem_limit_bytes=40 * 1024 * 1024),
+            name=name,
+        )(*args)
+
+    full_bf, full_f32 = shape((L, width), bf), shape((L, width), f32)
+    lin_out, gated, near, squares, cross = call(
+        forward_kernel,
+        "lightning_forward",
+        [
+            wide, wide, wide, wide,
+            pl.BlockSpec((1, DH), lambda h: (0, h)),
+            row_spec, col_spec, state_spec,
+            pl.BlockSpec(kv_grads.shape, lambda h: (0, 0, 0, 0)),
+            pl.BlockSpec((H, 2, DH, kc), lambda h: (0, 0, h, 0)),
+        ],
+        [
+            (wide, full_f32), (wide, full_f32), (square_spec, shape((hl, L, L), bf)),
+            (sum_spec, shape((L, 1), f32)), (sum_spec, shape((L, 1), f32)),
+        ],
+        2 * L * DH * (2 * L + DH + 2 * H * kc),
+        lin_query, lin_keys, lin_values, lin_grad, norm_gain[None, :], row, col, state_in,
+        kv_grads, projected,
+    )
+    squares, cross = lax.psum((squares[:, 0], cross[:, 0]), "head")
+    dout, summary = call(
+        norm_kernel,
+        "norm_backward",
+        [wide, wide, sum_spec, sum_spec, wide, col_spec],
+        [(wide, full_bf), (matrix_spec, shape((hl, DH, DH), bf))],
+        2 * L * DH * DH,
+        lin_out, gated, squares[:, None], cross[:, None], lin_query, col,
+    )
+    after = later_states(summary, starts)
+    lin_dq, part_key, part_value = call(
+        inner_kernel,
+        "lightning_inner",
+        [wide, wide, wide, wide, square_spec, state_spec, row_spec, col_spec],
+        [(wide, full_bf), (wide, full_f32), (wide, full_f32)],
+        2 * L * DH * (4 * L + DH),
+        lin_query, lin_keys, lin_values, dout, near, state_in, row, col,
+    )
+    lin_dk, lin_dv = call(
+        outer_kernel,
+        "lightning_outer",
+        [wide, wide, wide, wide, col_spec, matrix_spec],
+        [(wide, full_bf), (wide, full_bf)],
+        4 * L * DH * DH,
+        lin_keys, lin_values, part_key, part_value, col, after,
+    )
+    return lin_dq, lin_dk, lin_dv
 
 
 def per_device(
@@ -380,12 +491,8 @@
     soft_dq, soft_dk, soft_dv, kv_grads, projected = softmax_part(
         soft_query, soft_keys, soft_values, soft_grad, projections, doc_lengths
     )
-    carried_back = jnp.einsum(
-        "hctk,hcfk->tf", kv_grads, projected, preferred_element_type=jnp.float32
-    )
-    cotangent = lin_grad.astype(jnp.float32) + carried_back
     lin_dq, lin_dk, lin_dv = lightning_part(
-        lin_query, lin_keys, lin_values, cotangent, norm_gain, log_decay, state_in
+        lin_query, lin_keys, lin_values, lin_grad, norm_gain, log_decay, state_in, kv_grads, projected
     )
     return (lin_dq, lin_dk, lin_dv, soft_dq, soft_dk, soft_dv)
 

time: 324 us -> 256 us (0.79)
  waiting for transfers between devices: 98.8 us -> 3.05 us
  matrix products: 40.8 us -> 0 us
  Pallas kernels: 136 us -> 175 us
  other arithmetic: 5.67 us -> 20.7 us
  starting transfers between devices: 0.04 us -> 14.3 us
  local copies, waits for them, and re-layouts: 21.7 us -> 34.9 us
  between operations: 14.3 us -> 1.34 us
    all_gather x1 -> x0, waiting for transfers between devices: 98.8 us -> none  [lightning_part(): block_in = lax.all_gather(summary[None], 'ctx', axis=0, tiled=True)]
    dot_general x13 -> x0, matrix products: 40.8 us -> none  [the longest x1 12.3 us: lightning_part(): jnp.einsum('hn,nhde->hde', factors, block_in.astype(jnp.float32), precisi...]
    pallas_call x0 -> x4, Pallas kernels: none -> 39.8 us  [call(): pl.pallas_call(body, grid=(hl,), in_specs=ins, out_specs=tuple((spec for...]
    ppermute x0 -> x9, starting transfers between devices: none -> 14.3 us  [the longest x3 8.15 us: later_states(): lax.ppermute(whole, 'ctx', [(i, i - PLANE * e) for i in range(PLANE * e,...]
    unnamed x46 -> x102, local copies, waits for them, and re-layouts: 14.7 us -> 23.2 us
    gather x0 -> x2, local copies, waits for them, and re-layouts: none -> 3.83 us  [the longest x1 1.94 us: later_states(): to_level = jnp.take(local, target + 1, axis=1)]
    convert_element_type x1 -> x4, other arithmetic: 2.06 us -> 5.68 us  [the longest x3 3.94 us: later_states(): block = block.astype(jnp.bfloat16)]
    dot_general x1 -> x0, local copies, waits for them, and re-layouts: 3.47 us -> none  [lightning_part(): jnp.einsum('hn,nhde->hde', factors, block_in.astype(jnp.float32), precisi...]
  transfers between devices with their start and end apart: 1 -> 9, of which waited for: 1 -> 1; matrix products, arithmetic and copies ran while one was open for 3% -> 10% of each run, Pallas kernels for 0% -> 4%
where the time goes in v1:
time: 256 us; the launch traced here: 254 us
  Pallas kernels  175 us (68%)
  local copies, waits for them, and re-layouts  34.9 us (14%)
  other arithmetic  20.7 us (8%)
  starting transfers between devices  14.3 us (6%)
  blocking collectives  4.6 us (2%)
  waiting for transfers between devices  3.05 us (1%)
    pallas_call x1, Pallas kernels, softmax_part(): pl.pallas_call(functools.partial(soft_kernel, chain, heads), out_shape=(j...  136 us
    pallas_call x4, Pallas kernels, call(): pl.pallas_call(body, grid=(hl,), in_specs=ins, out_specs=tuple((spec for...  39.8 us
    unnamed x102, local copies, waits for them, and re-layouts  23.2 us
    ppermute x3, starting transfers between devices, later_states(): lax.ppermute(whole, 'ctx', [(i, i - PLANE * e) for i in range(PLANE * e,...  8.15 us
    ppermute x6, starting transfers between devices, within(): return lax.ppermute(block, 'ctx', route)  6.14 us
  transfers between devices with their start and end apart: 9, of which 1 were waited for; matrix products, arithmetic and copies ran while one was open for 10% of the time, Pallas kernels for 4%

profile of v1, /device:TPU:24, one launch (start us, length us, event | category | flops | bytes accessed | tf_op | source)
XLA Modules:
  0.0 254.2 jit_solution(14156118160409816852)
XLA Ops:
  2.3 2.0 reduce_window_sum.54.col
  4.8 0.9 fusion.kdoc
  6.3 135.5 %softmax_layer.1 = (bf16[256,4096]{1,0:T(8,128)(2,1)}, bf16[256,512]{1,0:T(8,128)(2,1)}, bf16[256,512]{1,0:T(8,128)(2,1)}, bf16[2,2,256,512]{3,2,1,0:T(8,128)(2,1)}, bf16[2,2,2048,512]{3,2,1,0:T(8,128)(2,1)}) custom-call(bf16[256,4096]{1,0:T(8,128)(2,1)} %q.4, bf16[256,4096]{1,0:T(8,128)(2,1)} %g.1, bf16[256,512]{1,0:T(8,128)(2,1)} %k.4, ...), custom_call_target="tpu_custom_call" | custom-call | tf_op jit(solution)/shard_map/softmax_layer/pallas_call | solution.py:242
  142.0 1.2 copy-done.19
  143.2 16.0 %lightning_forward.1 = (f32[256,2048]{1,0:T(8,128)S(1)}, f32[256,2048]{1,0:T(8,128)S(1)}, bf16[16,256,256]{2,1,0:T(8,128)(2,1)S(1)}, f32[256,1]{1,0:T(8,128)S(1)}, f32[256,1]{1,0:T(8,128)S(1)}) custom-call(bf16[256,2048]{1,0:T(8,128)(2,1)S(1)} %copy-done.3, bf16[256,2048]{1,0:T(8,128)(2,1)S(1)} %copy-done, bf16[256,2048]{1,0:T(8,128)(2,1)S(1)} %copy-done.1, ...), custom_call_target="tpu_custom_call" | custom-call | flops 2818572288 | bytes 8388608 | tf_op jit(solution)/shard_map/lightning_forward/pallas_call | solution.py:415
  159.2 1.4 copy-done.6
  160.5 1.3 copy-done.10
  161.8 1.3 copy-done.12
  163.2 4.6 %all-reduce.1 = (f32[256,1]{1,0:T(8,128)S(1)}, f32[256,1]{1,0:T(8,128)}) all-reduce(f32[256,1]{1,0:T(8,128)S(1)} %get-tuple-element.28, f32[256,1]{1,0:T(8,128)S(1)} %get-tuple-element.29), channel_id=1, replica_groups=mesh['ctx'=16,'head'=2] {'head'}, use_global_device_ids=true, to_apply=%region_5.6 | all-reduce | flops 512 | bytes 4096 | tf_op jit(solution)/shard_map/psum | solution.py:447
  167.8 1.2 copy-done.4
  169.0 1.6 copy-done.11
  170.6 1.6 copy-done.13
  172.2 0.9 copy-done.20
  173.1 6.2 %norm_backward.1 = (bf16[256,2048]{1,0:T(8,128)(2,1)S(1)}, bf16[16,128,128]{2,1,0:T(8,128)(2,1)S(1)}) custom-call(f32[256,2048]{1,0:T(8,128)S(1)} %copy-done.11, f32[256,2048]{1,0:T(8,128)S(1)} %copy-done.13, f32[256,1]{1,0:T(8,128)S(1)} %get-tuple-element.46.squares, f32[256,1]{1,0:T(8,128)S(1)} %copy-done.20, bf16[256,2048]{1,0:T(8,128)(2,1)S(1)} %copy-done.4, ...), custom_call_target="tpu_custom_call" | custom-call | flops 134217728 | bytes 8388608 | tf_op jit(solution)/shard_map/norm_backward/pallas_call | solution.py:415
  179.3 1.0 copy-done.17
  180.2 0.8 copy-done.14
  181.0 0.8 constant_dynamic-slice_fusion.2
  182.9 2.4 collective-permute-start.2
  187.0 1.7 copy.44
  188.7 1.7 reduce_sum.32
  190.4 1.5 reduce_window_sum.53
  191.8 1.3 pad_dynamic-slice_fusion.3
  193.1 1.3 copy.40
  194.4 1.3 pad_clamp_fusion
  195.7 1.2 pad_clamp_fusion.1
  196.9 1.9 gather_fusion.1
  198.8 1.9 gather_fusion
  201.5 1.6 fusion.37
  203.8 0.8 minimum_exponential_fusion.1
  205.3 1.7 fusion.4
  207.1 3.9 %collective-permute-start.3 = (bf16[4,128,128]{2,1,0:T(8,128)(2,1)}, bf16[4,128,128]{2,1,0:T(8,128)(2,1)}, u32[]{:S(2)}, u32[]{:S(2)}) collective-permute-start(bf16[4,128,128]{2,1,0:T(8,128)(2,1)} %fusion.4), channel_id=1, source_target_pairs={{8,0},{10,2},{12,4},{14,6},{16,8},{18,10},{20,12},{22,14},{24,16},... | collective-permute-start | bytes 393224 | tf_op jit(solution)/shard_map/ppermute | solution.py:371
  211.0 2.3 collective-permute-start.4
  213.3 1.9 collective-permute-start.5
  215.8 1.2 copy-done.2
  217.1 1.2 copy-done.5
  218.3 1.6 copy-done.7
  219.9 1.0 copy-done.9
  220.9 1.2 copy-done.18
  222.3 10.2 %lightning_inner.1 = (bf16[256,2048]{1,0:T(8,128)(2,1)}, f32[256,2048]{1,0:T(8,128)S(1)}, f32[256,2048]{1,0:T(8,128)S(1)}) custom-call(bf16[256,2048]{1,0:T(8,128)(2,1)S(1)} %copy-done.5, bf16[256,2048]{1,0:T(8,128)(2,1)S(1)} %copy-done, bf16[256,2048]{1,0:T(8,128)(2,1)S(1)} %copy-done.2, bf16[256,2048]{1,0:T(8,128)(2,1)S(1)} %copy-done.18, ...), custom_call_target="tpu_custom_call" | custom-call | flops 1207959552 | bytes 8388608 | tf_op jit(solution)/shard_map/lightning_inner/pallas_call | solution.py:415
  232.6 1.3 fusion.24
  234.0 1.3 fusion.19
  235.3 1.2 collective-permute-start.7
  236.6 1.3 fusion.14
  237.9 1.4 collective-permute-start.6
  239.4 1.3 fusion.25
  240.8 3.0 %collective-permute-done.6 = bf16[4,128,128]{2,1,0:T(8,128)(2,1)S(1)} collective-permute-done((bf16[4,128,128]{2,1,0:T(8,128)(2,1)S(1)}, bf16[4,128,128]{2,1,0:T(8,128)(2,1)S(1)}, u32[]{:S(2)}, u32[]{:S(2)}) %collective-permute-start.6) | collective-permute-done | bytes 131104 | tf_op jit(solution)/shard_map/ppermute | solution.py:346
  243.9 7.5 %lightning_outer.1 = (bf16[256,2048]{1,0:T(8,128)(2,1)}, bf16[256,2048]{1,0:T(8,128)(2,1)}) custom-call(bf16[256,2048]{1,0:T(8,128)(2,1)S(1)} %copy-done, bf16[256,2048]{1,0:T(8,128)(2,1)S(1)} %copy-done.2, f32[256,2048]{1,0:T(8,128)S(1)} %get-tuple-element.33.part_key, f32[256,2048]{1,0:T(8,128)S(1)} %get-tuple-element.34.part_value, ...), custom_call_target="tpu_custom_call" | custom-call | flops 268435456 | bytes 8388608 | tf_op jit(solution)/shard_map/lightning_outer/pallas_call | solution.py:415
  251.5 1.3 copy.53
  (122 shorter events, 10.1 us)
Async XLA Ops:
  0.6 3.7 %copy-start.48 = (s32[8]{0:T(128)S(1)}, s32[8]{0:T(128)}, u32[]{:S(2)}) copy-start(s32[8]{0:T(128)} %param.27) | copy-start | bytes 100
  6.3 135.6 %copy-start = (bf16[256,2048]{1,0:T(8,128)(2,1)S(1)}, bf16[256,2048]{1,0:T(8,128)(2,1)}, u32[]{:S(2)}) copy-start(bf16[256,2048]{1,0:T(8,128)(2,1)} %k.7) | copy-start | bytes 3145732
  6.3 135.6 %copy-start.1 = (bf16[256,2048]{1,0:T(8,128)(2,1)S(1)}, bf16[256,2048]{1,0:T(8,128)(2,1)}, u32[]{:S(2)}) copy-start(bf16[256,2048]{1,0:T(8,128)(2,1)} %v.7) | copy-start | bytes 3145732
  6.3 135.6 %copy-start.3 = (bf16[256,2048]{1,0:T(8,128)(2,1)S(1)}, bf16[256,2048]{1,0:T(8,128)(2,1)}, u32[]{:S(2)}) copy-start(bf16[256,2048]{1,0:T(8,128)(2,1)} %q.7) | copy-start | bytes 3145732
  6.3 135.6 %copy-start.8 = (bf16[1,16,128,128]{3,2,1,0:T(8,128)(2,1)S(1)}, bf16[1,16,128,128]{3,2,1,0:T(8,128)(2,1)}, u32[]{:S(2)}) copy-start(bf16[1,16,128,128]{3,2,1,0:T(8,128)(2,1)} %state.3) | copy-start | bytes 1572868
  6.3 135.6 %copy-start.16 = (bf16[256,2048]{1,0:T(8,128)(2,1)S(1)}, bf16[256,2048]{1,0:T(8,128)(2,1)}, u32[]{:S(2)}) copy-start(bf16[256,2048]{1,0:T(8,128)(2,1)} %lg.1) | copy-start | bytes 3145732
  6.3 135.6 %copy-start.21 = (f32[2048]{0:T(1024)S(1)}, f32[2048]{0:T(1024)}, u32[]{:S(2)}) copy-start(f32[2048]{0:T(1024)} %param.19) | copy-start | bytes 24580
  159.1 1.4 copy-start.6
  161.8 1.3 copy-start.12
  169.0 1.6 copy-start.11
  170.6 1.6 copy-start.13
  181.8 23.5 %collective-permute-start = (bf16[4,128,128]{2,1,0:T(8,128)(2,1)}, bf16[4,128,128]{2,1,0:T(8,128)(2,1)S(1)}, u32[]{:S(2)}, u32[]{:S(2)}) collective-permute-start(bf16[4,128,128]{2,1,0:T(8,128)(2,1)} %get-tuple-element.52), channel_id=1, source_target_pairs={{0,2},{2,4},{4,6},{6,0},{8,10},{10,12},{12,14},{14,8},{16,18},{18,... | collective-permute-start | bytes 393224 | tf_op jit(solution)/shard_map/ppermute | solution.py:346
  182.3 23.0 %collective-permute-start.1 = (bf16[4,128,128]{2,1,0:T(8,128)(2,1)}, bf16[4,128,128]{2,1,0:T(8,128)(2,1)S(1)}, u32[]{:S(2)}, u32[]{:S(2)}) collective-permute-start(bf16[4,128,128]{2,1,0:T(8,128)(2,1)} %get-tuple-element.54), channel_id=1, source_target_pairs={{0,4},{2,6},{4,0},{6,2},{8,12},{10,14},{12,8},{14,10},{16,20},{18,... | collective-permute-start | bytes 393224 | tf_op jit(solution)/shard_map/ppermute | solution.py:346
  182.9 22.5 %collective-permute-start.2 = (bf16[4,128,128]{2,1,0:T(8,128)(2,1)}, bf16[4,128,128]{2,1,0:T(8,128)(2,1)S(1)}, u32[]{:S(2)}, u32[]{:S(2)}) collective-permute-start(bf16[4,128,128]{2,1,0:T(8,128)(2,1)} %get-tuple-element.53), channel_id=1, source_target_pairs={{0,6},{2,0},{4,2},{6,4},{8,14},{10,8},{12,10},{14,12},{16,22},{18,... | collective-permute-start | bytes 393224 | tf_op jit(solution)/shard_map/ppermute | solution.py:346
  207.1 25.4 %collective-permute-start.3 = (bf16[4,128,128]{2,1,0:T(8,128)(2,1)}, bf16[4,128,128]{2,1,0:T(8,128)(2,1)}, u32[]{:S(2)}, u32[]{:S(2)}) collective-permute-start(bf16[4,128,128]{2,1,0:T(8,128)(2,1)} %fusion.4), channel_id=1, source_target_pairs={{8,0},{10,2},{12,4},{14,6},{16,8},{18,10},{20,12},{22,14},{24,16},... | collective-permute-start | bytes 393224 | tf_op jit(solution)/shard_map/ppermute | solution.py:371
  211.0 21.5 %collective-permute-start.4 = (bf16[4,128,128]{2,1,0:T(8,128)(2,1)}, bf16[4,128,128]{2,1,0:T(8,128)(2,1)}, u32[]{:S(2)}, u32[]{:S(2)}) collective-permute-start(bf16[4,128,128]{2,1,0:T(8,128)(2,1)} %fusion.4), channel_id=1, source_target_pairs={{16,0},{18,2},{20,4},{22,6},{24,8},{26,10},{28,12},{30,14},{17,1},... | collective-permute-start | bytes 393224 | tf_op jit(solution)/shard_map/ppermute | solution.py:371
  213.3 19.2 %collective-permute-start.5 = (bf16[4,128,128]{2,1,0:T(8,128)(2,1)}, bf16[4,128,128]{2,1,0:T(8,128)(2,1)}, u32[]{:S(2)}, u32[]{:S(2)}) collective-permute-start(bf16[4,128,128]{2,1,0:T(8,128)(2,1)} %fusion.4), channel_id=1, source_target_pairs={{24,0},{26,2},{28,4},{30,6},{25,1},{27,3},{29,5},{31,7}} | collective-permute-start | bytes 393224 | tf_op jit(solution)/shard_map/ppermute | solution.py:371
  218.3 1.6 copy-start.7
  222.1 10.4 %copy-start.15 = (bf16[16,128,128]{2,1,0:T(8,128)(2,1)S(1)}, bf16[16,128,128]{2,1,0:T(8,128)(2,1)}, u32[]{:S(2)}) copy-start(bf16[16,128,128]{2,1,0:T(8,128)(2,1)} %copy-done.14) | copy-start | bytes 1572868
  222.1 10.4 %copy-start.25 = (f32[4]{0:T(128)S(1)}, f32[4]{0:T(128)}, u32[]{:S(2)}) copy-start(f32[4]{0:T(128)} %get-tuple-element.41) | copy-start | bytes 52
  222.1 10.4 %copy-start.26 = (f32[4]{0:T(128)S(1)}, f32[4]{0:T(128)}, u32[]{:S(2)}) copy-start(f32[4]{0:T(128)} %get-tuple-element.42) | copy-start | bytes 52
  222.1 10.4 %copy-start.27 = (f32[4]{0:T(128)S(1)}, f32[4]{0:T(128)}, u32[]{:S(2)}) copy-start(f32[4]{0:T(128)} %get-tuple-element.43) | copy-start | bytes 52
  222.1 10.4 %copy-start.41 = (f32[4]{0:T(128)S(1)}, f32[4]{0:T(128)}, u32[]{:S(2)}) copy-start(f32[4]{0:T(128)} %get-tuple-element.55) | copy-start | bytes 52
  222.2 10.4 %copy-start.42 = (f32[4]{0:T(128)S(1)}, f32[4]{0:T(128)}, u32[]{:S(2)}) copy-start(f32[4]{0:T(128)} %get-tuple-element.56) | copy-start | bytes 52
  222.2 10.4 %copy-start.43 = (f32[4]{0:T(128)S(1)}, f32[4]{0:T(128)}, u32[]{:S(2)}) copy-start(f32[4]{0:T(128)} %get-tuple-element.57) | copy-start | bytes 52
  222.2 10.4 %copy-start.44 = (f32[4]{0:T(128)S(1)}, f32[4]{0:T(128)}, u32[]{:S(2)}) copy-start(f32[4]{0:T(128)} %get-tuple-element.58) | copy-start | bytes 52
  222.2 10.4 %copy-start.47 = (f32[4]{0:T(128)S(1)}, f32[4]{0:T(128)}, u32[]{:S(2)}) copy-start(f32[4]{0:T(128)} %get-tuple-element.71) | copy-start | bytes 52
  222.2 11.8 %copy-start.37 = (f32[4]{0:T(128)S(1)}, f32[4]{0:T(128)}, u32[]{:S(2)}) copy-start(f32[4]{0:T(128)} %get-tuple-element.59) | copy-start | bytes 52
  222.2 11.8 %copy-start.38 = (f32[4]{0:T(128)S(1)}, f32[4]{0:T(128)}, u32[]{:S(2)}) copy-start(f32[4]{0:T(128)} %get-tuple-element.60) | copy-start | bytes 52
  222.2 11.8 %copy-start.39 = (f32[4]{0:T(128)S(1)}, f32[4]{0:T(128)}, u32[]{:S(2)}) copy-start(f32[4]{0:T(128)} %get-tuple-element.61) | copy-start | bytes 52
  222.2 11.8 %copy-start.40 = (f32[4]{0:T(128)S(1)}, f32[4]{0:T(128)}, u32[]{:S(2)}) copy-start(f32[4]{0:T(128)} %get-tuple-element.62) | copy-start | bytes 52
  222.2 11.8 %copy-start.46 = (f32[4]{0:T(128)S(1)}, f32[4]{0:T(128)}, u32[]{:S(2)}) copy-start(f32[4]{0:T(128)} %get-tuple-element.72) | copy-start | bytes 52
  232.4 4.1 %copy-start.33 = (f32[4]{0:T(128)S(1)}, f32[4]{0:T(128)}, u32[]{:S(2)}) copy-start(f32[4]{0:T(128)} %get-tuple-element.63) | copy-start | bytes 52
  232.4 4.1 %copy-start.34 = (f32[4]{0:T(128)S(1)}, f32[4]{0:T(128)}, u32[]{:S(2)}) copy-start(f32[4]{0:T(128)} %get-tuple-element.64) | copy-start | bytes 52
  232.4 4.1 %copy-start.35 = (f32[4]{0:T(128)S(1)}, f32[4]{0:T(128)}, u32[]{:S(2)}) copy-start(f32[4]{0:T(128)} %get-tuple-element.65) | copy-start | bytes 52
  232.4 4.1 %copy-start.36 = (f32[4]{0:T(128)S(1)}, f32[4]{0:T(128)}, u32[]{:S(2)}) copy-start(f32[4]{0:T(128)} %get-tuple-element.66) | copy-start | bytes 52
  232.4 4.1 %copy-start.45 = (f32[4]{0:T(128)S(1)}, f32[4]{0:T(128)}, u32[]{:S(2)}) copy-start(f32[4]{0:T(128)} %get-tuple-element.73) | copy-start | bytes 52
  232.4 7.0 %copy-start.28 = (f32[4]{0:T(128)S(1)}, f32[4]{0:T(128)}, u32[]{:S(2)}) copy-start(f32[4]{0:T(128)} %get-tuple-element.67) | copy-start | bytes 52
  232.4 7.0 %copy-start.29 = (f32[4]{0:T(128)S(1)}, f32[4]{0:T(128)}, u32[]{:S(2)}) copy-start(f32[4]{0:T(128)} %get-tuple-element.68) | copy-start | bytes 52
  232.4 7.0 %copy-start.30 = (f32[4]{0:T(128)S(1)}, f32[4]{0:T(128)}, u32[]{:S(2)}) copy-start(f32[4]{0:T(128)} %get-tuple-element.69) | copy-start | bytes 52
  232.5 7.0 %copy-start.31 = (f32[4]{0:T(128)S(1)}, f32[4]{0:T(128)}, u32[]{:S(2)}) copy-start(f32[4]{0:T(128)} %get-tuple-element.70) | copy-start | bytes 52
  232.5 7.0 %copy-start.32 = (f32[4]{0:T(128)S(1)}, f32[4]{0:T(128)}, u32[]{:S(2)}) copy-start(f32[4]{0:T(128)} %get-tuple-element.74) | copy-start | bytes 52
  233.9 10.0 %collective-permute-start.8 = (bf16[4,128,128]{2,1,0:T(8,128)(2,1)S(1)}, bf16[4,128,128]{2,1,0:T(8,128)(2,1)S(1)}, u32[]{:S(2)}, u32[]{:S(2)}) collective-permute-start(bf16[4,128,128]{2,1,0:T(8,128)(2,1)S(1)} %fusion.24), channel_id=1, source_target_pairs={{0,6},{2,0},{4,2},{6,4},{8,14},{10,8},{12,10},{14,12},{16,22},{18,... | collective-permute-start | bytes 393224 | tf_op jit(solution)/shard_map/ppermute | solution.py:346
  235.3 8.5 %collective-permute-start.7 = (bf16[4,128,128]{2,1,0:T(8,128)(2,1)S(1)}, bf16[4,128,128]{2,1,0:T(8,128)(2,1)S(1)}, u32[]{:S(2)}, u32[]{:S(2)}) collective-permute-start(bf16[4,128,128]{2,1,0:T(8,128)(2,1)S(1)} %fusion.19), channel_id=1, source_target_pairs={{0,4},{2,6},{4,0},{6,2},{8,12},{10,14},{12,8},{14,10},{16,20},{18,... | collective-permute-start | bytes 393224 | tf_op jit(solution)/shard_map/ppermute | solution.py:346
  237.9 5.9 %collective-permute-start.6 = (bf16[4,128,128]{2,1,0:T(8,128)(2,1)S(1)}, bf16[4,128,128]{2,1,0:T(8,128)(2,1)S(1)}, u32[]{:S(2)}, u32[]{:S(2)}) collective-permute-start(bf16[4,128,128]{2,1,0:T(8,128)(2,1)S(1)} %fusion.14), channel_id=1, source_target_pairs={{0,2},{2,4},{4,6},{6,0},{8,10},{10,12},{12,14},{14,8},{16,18},{18,... | collective-permute-start | bytes 393224 | tf_op jit(solution)/shard_map/ppermute | solution.py:346
  243.9 7.6 %copy-start.22 = (bf16[256,4096]{1,0:T(8,128)(2,1)S(1)}, bf16[256,4096]{1,0:T(8,128)(2,1)}, u32[]{:S(2)}) copy-start(bf16[256,4096]{1,0:T(8,128)(2,1)} %get-tuple-element.94) | copy-start | bytes 6291460
  251.5 1.3 copy-start.24
  251.5 2.0 copy-start.23
  (10 other events, 11.2 us)

commit v2 on v1

--- a/solution.py
+++ b/solution.py
@@ -13,7 +13,8 @@
 KV_HEADS = 8
 LIGHTNING_HEADS = 32
 SUB = 4
-PAIR = 2
+PAIR = 4
+CHAIN = 2
 
 epsilon = 1e-06
 MESH = pl.DeviceIdType.MESH
@@ -152,16 +153,23 @@
             k_win = win[0, c, pl.ds(r, W), :]
             v_win = win[1, c, pl.ds(r, W), :]
             b = bias[half]
-            s = mm(k_win, q_rows, LAST) * to_base2 + jnp.concatenate([b] * PAIR, 1)
-            m = jnp.max(s, axis=0, keepdims=True)
-            e = jnp.exp2(s - m)
-            total = jnp.sum(e, axis=0, keepdims=True)
-            dp = mm(v_win, g_rows, LAST)
-            inv = 1.0 / total
-            delta = jnp.sum(e * dp, axis=0, keepdims=True) * inv
-            p = e * inv
-            p_low = p.astype(jnp.bfloat16)
-            ds = (p * (dp - delta)).astype(jnp.bfloat16)
+            width = half_rows * CHAIN
+            chains = range(0, half_rows * PAIR, width)
+            bias_wide = jnp.concatenate([b] * CHAIN, 1)
+            scores = [mm(k_win, q_rows[x : x + width], LAST) for x in chains]
+            grads = [mm(v_win, g_rows[x : x + width], LAST) for x in chains]
+            ds_parts, p_parts = [], []
+            for score, dp in zip(scores, grads):
+                s = score * to_base2 + bias_wide
+                m = jnp.max(s, axis=0, keepdims=True)
+                e = jnp.exp2(s - m)
+                inv = 1.0 / jnp.sum(e, axis=0, keepdims=True)
+                delta = jnp.sum(e * dp, axis=0, keepdims=True) * inv
+                p = e * inv
+                p_parts.append(p.astype(jnp.bfloat16))
+                ds_parts.append((p * (dp - delta)).astype(jnp.bfloat16))
+            ds = jnp.concatenate(ds_parts, 1)
+            p_low = jnp.concatenate(p_parts, 1)
             acc[0, pl.ds(r, W), :] += mm(ds, q_rows, PLAIN)
             acc[1, pl.ds(r, W), :] += mm(p_low, g_rows, PLAIN)
             dq_t = mm(k_win, ds, FIRST) * score_scale
@@ -334,7 +342,7 @@
 PLANE = 4
 
 
-def later_states(summary, starts):
+def later_states(summary, totals):
     chain = lax.axis_size("ctx")
     groups = chain // PLANE
     me = lax.axis_index("ctx")
@@ -352,18 +360,32 @@
     for d in range(1, PLANE):
         pieces.append(within(quarter(summary, (j + d) % PLANE), d))
     pieces = [piece.astype(jnp.float32) for piece in pieces]
-    levels = quarter(starts, j)
-    local = lax.dynamic_slice_in_dim(levels, z * PLANE, PLANE + 1, 1)
-    source = (j - jnp.arange(PLANE)) % PLANE
-    target = (j + jnp.arange(PLANE)) % PLANE
-    from_level = jnp.take(local, source, axis=1)
-    to_level = jnp.take(local, target + 1, axis=1)
-    to_first = jnp.exp(jnp.minimum(from_level - local[:, :1], 0.0))
-    factors = jnp.where(
-        source[None, :, None] > target[None, None, :],
-        jnp.exp(jnp.minimum(from_level[:, :, None] - to_level[:, None, :], 0.0)),
-        0.0,
-    )
+    ring = jnp.arange(PLANE, dtype=jnp.int32)
+    first = z * PLANE
+    source = first + (j - ring) % PLANE
+    target = first + (j + ring) % PLANE
+    beyond = first + PLANE
+    farther = beyond + PLANE * jnp.arange(groups, dtype=jnp.int32)
+    begins = jnp.concatenate(
+        [
+            jnp.tile(target + 1, PLANE),
+            jnp.full((PLANE,), first),
+            target + 1,
+            jnp.full((groups,), beyond),
+        ]
+    )
+    ends = jnp.concatenate(
+        [jnp.repeat(source, PLANE), source, jnp.full((PLANE,), beyond), farther]
+    )
+    block = jnp.arange(chain, dtype=jnp.int32)[:, None]
+    inside = ((block >= begins) & (block < ends)).astype(jnp.float32)
+    log_gap = jnp.sum(quarter(totals, j)[:, :, None] * inside[None], axis=1)
+    levels = jnp.where(ends >= begins, jnp.exp(log_gap), 0.0)
+    squared = PLANE * PLANE
+    factors = levels[:, :squared].reshape(part, PLANE, PLANE)
+    to_first = levels[:, squared : squared + PLANE]
+    last = levels[:, squared + PLANE : squared + 2 * PLANE]
+    decays = levels[:, squared + 2 * PLANE :]
     whole = sum(to_first[:, d, None, None] * pieces[d] for d in range(PLANE))
     whole = whole.astype(jnp.bfloat16)
     carry = jnp.zeros(whole.shape, jnp.float32)
@@ -371,10 +393,8 @@
         arrived = lax.ppermute(
             whole, "ctx", [(i, i - PLANE * e) for i in range(PLANE * e, chain)]
         )
-        level = lax.dynamic_slice_in_dim(levels, jnp.minimum((z + e) * PLANE, chain), 1, 1)
-        decay = jnp.exp(jnp.minimum(level - local[:, PLANE:], 0.0))
+        decay = decays[:, e - 1 : e]
         carry = carry + decay[:, :, None] * arrived.astype(jnp.float32)
-    last = jnp.exp(jnp.minimum(local[:, PLANE:] - to_level, 0.0))
     result = jnp.zeros(summary.shape, jnp.bfloat16)
     for d in range(PLANE):
         block = last[:, d, None, None] * carry
@@ -397,9 +417,6 @@
     running = jnp.cumsum(log_block, axis=1)
     row, col = running[:, None, :], running[:, :, None]
     totals = jnp.sum(log_decay.reshape(hl, chain, L), axis=2)
-    starts = jnp.concatenate(
-        [jnp.zeros((hl, 1), jnp.float32), jnp.cumsum(totals, axis=1)], axis=1
-    )
     bf, f32 = jnp.bfloat16, jnp.float32
     H, _, _, kc = kv_grads.shape
     wide = pl.BlockSpec((L, DH), lambda h: (0, h))
@@ -453,7 +470,7 @@
         2 * L * DH * DH,
         lin_out, gated, squares[:, None], cross[:, None], lin_query, col,
     )
-    after = later_states(summary, starts)
+    after = later_states(summary, totals)
     lin_dq, part_key, part_value = call(
         inner_kernel,
         "lightning_inner",

time: 256 us -> 253 us (0.988)
  other arithmetic: 20.7 us -> 16.1 us
    gather x2 -> x0, local copies, waits for them, and re-layouts: 3.83 us -> none  [the longest x1 1.94 us: later_states(): to_level = jnp.take(local, target + 1, axis=1)]
    exp x3 -> x0, other arithmetic: 3.09 us -> none  [the longest x1 1.63 us: later_states(): decay = jnp.exp(jnp.minimum(level - local[:, PLANE:], 0.0))]
    dynamic_slice x2 -> x0, local copies, waits for them, and re-layouts: 2.6 us -> none  [later_states(): local = lax.dynamic_slice_in_dim(levels, z * PLANE, PLANE + 1, 1)]
    unnamed x102 -> x70, local copies, waits for them, and re-layouts: 23.2 us -> 25.7 us
  transfers between devices with their start and end apart: 9 -> 9, of which waited for: 1 -> 1; matrix products, arithmetic and copies ran while one was open for 10% -> 8% of each run, Pallas kernels for 4% -> 4%
where the time goes in v2:
time: 253 us; the launch traced here: 252 us
  Pallas kernels  175 us (69%)
  local copies, waits for them, and re-layouts  37.3 us (15%)
  other arithmetic  16.1 us (6%)
  starting transfers between devices  14.3 us (6%)
  blocking collectives  4.6 us (2%)
  waiting for transfers between devices  3.01 us (1%)
    pallas_call x1, Pallas kernels, softmax_part(): pl.pallas_call(functools.partial(soft_kernel, chain, heads), out_shape=(j...  136 us
    pallas_call x4, Pallas kernels, call(): pl.pallas_call(body, grid=(hl,), in_specs=ins, out_specs=tuple((spec for...  39.8 us
    unnamed x70, local copies, waits for them, and re-layouts  25.7 us
    ppermute x3, starting transfers between devices, later_states(): lax.ppermute(whole, 'ctx', [(i, i - PLANE * e) for i in range(PLANE * e,...  8.16 us
    ppermute x6, starting transfers between devices, within(): return lax.ppermute(block, 'ctx', route)  6.15 us
  transfers between devices with their start and end apart: 9, of which 1 were waited for; matrix products, arithmetic and copies ran while one was open for 8% of the time, Pallas kernels for 4%

profile of v2, /device:TPU:24, one launch (start us, length us, event | category | flops | bytes accessed | tf_op | source)
XLA Modules:
  0.0 251.8 jit_solution(11406038961993166939)
XLA Ops:
  2.3 2.0 reduce_window_sum.42.col
  4.8 0.9 fusion.kdoc
  6.3 135.6 %softmax_layer.1 = (bf16[256,4096]{1,0:T(8,128)(2,1)}, bf16[256,512]{1,0:T(8,128)(2,1)}, bf16[256,512]{1,0:T(8,128)(2,1)}, bf16[2,2,256,512]{3,2,1,0:T(8,128)(2,1)}, bf16[2,2,2048,512]{3,2,1,0:T(8,128)(2,1)}) custom-call(bf16[256,4096]{1,0:T(8,128)(2,1)} %q.4, bf16[256,4096]{1,0:T(8,128)(2,1)} %g.1, bf16[256,512]{1,0:T(8,128)(2,1)} %k.4, ...), custom_call_target="tpu_custom_call" | custom-call | tf_op jit(solution)/shard_map/softmax_layer/pallas_call | solution.py:250
  142.0 1.2 copy-done.23
  143.2 15.9 %lightning_forward.1 = (f32[256,2048]{1,0:T(8,128)S(1)}, f32[256,2048]{1,0:T(8,128)S(1)}, bf16[16,256,256]{2,1,0:T(8,128)(2,1)S(1)}, f32[256,1]{1,0:T(8,128)S(1)}, f32[256,1]{1,0:T(8,128)S(1)}) custom-call(bf16[256,2048]{1,0:T(8,128)(2,1)S(1)} %copy-done.4, bf16[256,2048]{1,0:T(8,128)(2,1)S(1)} %copy-done, bf16[256,2048]{1,0:T(8,128)(2,1)S(1)} %copy-done.1, ...), custom_call_target="tpu_custom_call" | custom-call | flops 2818572288 | bytes 8388608 | tf_op jit(solution)/shard_map/lightning_forward/pallas_call | solution.py:432
  159.2 1.3 copy-done.11
  160.6 1.3 copy-done.15
  161.9 1.3 copy-done.17
  163.2 4.6 %all-reduce = (f32[256,1]{1,0:T(8,128)S(1)}, f32[256,1]{1,0:T(8,128)}) all-reduce(f32[256,1]{1,0:T(8,128)S(1)} %get-tuple-element.27, f32[256,1]{1,0:T(8,128)S(1)} %get-tuple-element.28), channel_id=1, replica_groups=mesh['ctx'=16,'head'=2] {'head'}, use_global_device_ids=true, to_apply=%region_5.6 | all-reduce | flops 512 | bytes 4096 | tf_op jit(solution)/shard_map/psum | solution.py:464
  167.8 1.2 copy-done.5
  169.0 1.6 copy-done.16
  170.6 1.6 copy-done.18
  172.2 0.9 copy-done.24
  173.1 6.2 %norm_backward.1 = (bf16[256,2048]{1,0:T(8,128)(2,1)S(1)}, bf16[16,128,128]{2,1,0:T(8,128)(2,1)S(1)}) custom-call(f32[256,2048]{1,0:T(8,128)S(1)} %copy-done.16, f32[256,2048]{1,0:T(8,128)S(1)} %copy-done.18, f32[256,1]{1,0:T(8,128)S(1)} %get-tuple-element.67.squares, f32[256,1]{1,0:T(8,128)S(1)} %copy-done.24, bf16[256,2048]{1,0:T(8,128)(2,1)S(1)} %copy-done.5, ...), custom_call_target="tpu_custom_call" | custom-call | flops 134217728 | bytes 8388608 | tf_op jit(solution)/shard_map/norm_backward/pallas_call | solution.py:432
  179.3 1.0 copy-done.21
  180.3 0.8 copy-done.19
  181.0 0.8 constant_dynamic-slice_fusion.2
  182.9 2.4 collective-permute-start.2
  185.9 1.2 broadcast_in_dim.56
  187.1 1.3 reshape.194
  188.4 1.2 tile.4
  189.6 1.3 tile.10
  191.4 1.7 copy.48
  193.2 1.6 reduce_sum.41
  194.8 1.3 fusion.33
  197.4 0.8 multiply_reduce_fusion
  198.8 0.9 slice_reduce_fusion.17
  199.7 1.7 fusion.4
  201.4 4.0 %collective-permute-start.3 = (bf16[4,128,128]{2,1,0:T(8,128)(2,1)}, bf16[4,128,128]{2,1,0:T(8,128)(2,1)}, u32[]{:S(2)}, u32[]{:S(2)}) collective-permute-start(bf16[4,128,128]{2,1,0:T(8,128)(2,1)} %fusion.4), channel_id=1, source_target_pairs={{8,0},{10,2},{12,4},{14,6},{16,8},{18,10},{20,12},{22,14},{24,16},... | collective-permute-start | bytes 393224 | tf_op jit(solution)/shard_map/ppermute | solution.py:393
  205.4 2.2 collective-permute-start.4
  207.6 1.9 collective-permute-start.5
  209.5 1.2 copy-done.2
  210.8 1.2 copy-done.6
  212.0 1.6 copy-done.12
  213.6 1.0 copy-done.14
  214.6 1.2 copy-done.22
  215.9 10.1 %lightning_inner.1 = (bf16[256,2048]{1,0:T(8,128)(2,1)}, f32[256,2048]{1,0:T(8,128)S(1)}, f32[256,2048]{1,0:T(8,128)S(1)}) custom-call(bf16[256,2048]{1,0:T(8,128)(2,1)S(1)} %copy-done.6, bf16[256,2048]{1,0:T(8,128)(2,1)S(1)} %copy-done, bf16[256,2048]{1,0:T(8,128)(2,1)S(1)} %copy-done.2, bf16[256,2048]{1,0:T(8,128)(2,1)S(1)} %copy-done.22, ...), custom_call_target="tpu_custom_call" | custom-call | flops 1207959552 | bytes 8388608 | tf_op jit(solution)/shard_map/lightning_inner/pallas_call | solution.py:432
  226.0 1.3 copy-done.7
  227.3 1.3 copy-done.9
  229.7 1.5 fusion.24
  231.3 1.5 fusion.19
  232.9 1.2 collective-permute-start.7
  234.1 1.4 fusion.14
  235.4 1.4 collective-permute-start.6
  237.0 1.4 fusion.25
  238.4 3.0 %collective-permute-done.6 = bf16[4,128,128]{2,1,0:T(8,128)(2,1)S(1)} collective-permute-done((bf16[4,128,128]{2,1,0:T(8,128)(2,1)S(1)}, bf16[4,128,128]{2,1,0:T(8,128)(2,1)S(1)}, u32[]{:S(2)}, u32[]{:S(2)}) %collective-permute-start.6) | collective-permute-done | bytes 131104 | tf_op jit(solution)/shard_map/ppermute | solution.py:354
  241.5 7.5 %lightning_outer.1 = (bf16[256,2048]{1,0:T(8,128)(2,1)}, bf16[256,2048]{1,0:T(8,128)(2,1)}) custom-call(bf16[256,2048]{1,0:T(8,128)(2,1)S(1)} %copy-done, bf16[256,2048]{1,0:T(8,128)(2,1)S(1)} %copy-done.3, f32[256,2048]{1,0:T(8,128)S(1)} %copy-done.8, f32[256,2048]{1,0:T(8,128)S(1)} %copy-done.10, f32[16,256,1]{2,1,0:T(8,128)S(1)} %reduce_window_sum.42.col, ...), custom_call_target="tpu_custom_call" | custom-call | flops 268435456 | bytes 8388608 | tf_op jit(solution)/shard_map/lightning_outer/pallas_call | solution.py:432
  249.1 1.3 copy.57
  (88 shorter events, 9.6 us)
Async XLA Ops:
  0.6 3.7 %copy-start.32 = (s32[8]{0:T(128)S(1)}, s32[8]{0:T(128)}, u32[]{:S(2)}) copy-start(s32[8]{0:T(128)} %param.25) | copy-start | bytes 100
  6.3 135.6 %copy-start = (bf16[256,2048]{1,0:T(8,128)(2,1)S(1)}, bf16[256,2048]{1,0:T(8,128)(2,1)}, u32[]{:S(2)}) copy-start(bf16[256,2048]{1,0:T(8,128)(2,1)} %k.7) | copy-start | bytes 3145732
  6.3 135.7 %copy-start.1 = (bf16[256,2048]{1,0:T(8,128)(2,1)S(1)}, bf16[256,2048]{1,0:T(8,128)(2,1)}, u32[]{:S(2)}) copy-start(bf16[256,2048]{1,0:T(8,128)(2,1)} %v.7) | copy-start | bytes 3145732
  6.3 135.7 %copy-start.4 = (bf16[256,2048]{1,0:T(8,128)(2,1)S(1)}, bf16[256,2048]{1,0:T(8,128)(2,1)}, u32[]{:S(2)}) copy-start(bf16[256,2048]{1,0:T(8,128)(2,1)} %q.7) | copy-start | bytes 3145732
  6.3 135.7 %copy-start.13 = (bf16[1,16,128,128]{3,2,1,0:T(8,128)(2,1)S(1)}, bf16[1,16,128,128]{3,2,1,0:T(8,128)(2,1)}, u32[]{:S(2)}) copy-start(bf16[1,16,128,128]{3,2,1,0:T(8,128)(2,1)} %state.3) | copy-start | bytes 1572868
  6.3 135.7 %copy-start.20 = (bf16[256,2048]{1,0:T(8,128)(2,1)S(1)}, bf16[256,2048]{1,0:T(8,128)(2,1)}, u32[]{:S(2)}) copy-start(bf16[256,2048]{1,0:T(8,128)(2,1)} %lg.1) | copy-start | bytes 3145732
  6.3 135.7 %copy-start.25 = (f32[2048]{0:T(1024)S(1)}, f32[2048]{0:T(1024)}, u32[]{:S(2)}) copy-start(f32[2048]{0:T(1024)} %param.17) | copy-start | bytes 24580
  142.0 1.2 copy-start.23
  159.2 1.4 copy-start.11
  160.6 1.3 copy-start.15
  161.9 1.3 copy-start.17
  167.8 1.2 copy-start.5
  169.0 1.6 copy-start.16
  170.6 1.6 copy-start.18
  172.2 0.9 copy-start.24
  179.3 1.0 copy-start.21
  180.2 0.8 copy-start.19
  181.8 17.8 %collective-permute-start = (bf16[4,128,128]{2,1,0:T(8,128)(2,1)}, bf16[4,128,128]{2,1,0:T(8,128)(2,1)S(1)}, u32[]{:S(2)}, u32[]{:S(2)}) collective-permute-start(bf16[4,128,128]{2,1,0:T(8,128)(2,1)} %get-tuple-element.72), channel_id=1, source_target_pairs={{0,2},{2,4},{4,6},{6,0},{8,10},{10,12},{12,14},{14,8},{16,18},{18,... | collective-permute-start | bytes 393224 | tf_op jit(solution)/shard_map/ppermute | solution.py:354
  182.4 17.3 %collective-permute-start.1 = (bf16[4,128,128]{2,1,0:T(8,128)(2,1)}, bf16[4,128,128]{2,1,0:T(8,128)(2,1)S(1)}, u32[]{:S(2)}, u32[]{:S(2)}) collective-permute-start(bf16[4,128,128]{2,1,0:T(8,128)(2,1)} %get-tuple-element.74), channel_id=1, source_target_pairs={{0,4},{2,6},{4,0},{6,2},{8,12},{10,14},{12,8},{14,10},{16,20},{18,... | collective-permute-start | bytes 393224 | tf_op jit(solution)/shard_map/ppermute | solution.py:354
  182.9 16.7 %collective-permute-start.2 = (bf16[4,128,128]{2,1,0:T(8,128)(2,1)}, bf16[4,128,128]{2,1,0:T(8,128)(2,1)S(1)}, u32[]{:S(2)}, u32[]{:S(2)}) collective-permute-start(bf16[4,128,128]{2,1,0:T(8,128)(2,1)} %get-tuple-element.73), channel_id=1, source_target_pairs={{0,6},{2,0},{4,2},{6,4},{8,14},{10,8},{12,10},{14,12},{16,22},{18,... | collective-permute-start | bytes 393224 | tf_op jit(solution)/shard_map/ppermute | solution.py:354
  198.8 10.8 %copy-start.27 = (f32[4,28]{1,0:T(4,128)}, f32[4,28]{1,0:T(4,128)S(1)}, u32[]{:S(2)}) copy-start(f32[4,28]{1,0:T(4,128)S(1)} %exponential_select_fusion) | copy-start | bytes 1348
  201.4 28.3 %collective-permute-start.3 = (bf16[4,128,128]{2,1,0:T(8,128)(2,1)}, bf16[4,128,128]{2,1,0:T(8,128)(2,1)}, u32[]{:S(2)}, u32[]{:S(2)}) collective-permute-start(bf16[4,128,128]{2,1,0:T(8,128)(2,1)} %fusion.4), channel_id=1, source_target_pairs={{8,0},{10,2},{12,4},{14,6},{16,8},{18,10},{20,12},{22,14},{24,16},... | collective-permute-start | bytes 393224 | tf_op jit(solution)/shard_map/ppermute | solution.py:393
  205.4 24.3 %collective-permute-start.4 = (bf16[4,128,128]{2,1,0:T(8,128)(2,1)}, bf16[4,128,128]{2,1,0:T(8,128)(2,1)}, u32[]{:S(2)}, u32[]{:S(2)}) collective-permute-start(bf16[4,128,128]{2,1,0:T(8,128)(2,1)} %fusion.4), channel_id=1, source_target_pairs={{16,0},{18,2},{20,4},{22,6},{24,8},{26,10},{28,12},{30,14},{17,1},... | collective-permute-start | bytes 393224 | tf_op jit(solution)/shard_map/ppermute | solution.py:393
  207.6 22.1 %collective-permute-start.5 = (bf16[4,128,128]{2,1,0:T(8,128)(2,1)}, bf16[4,128,128]{2,1,0:T(8,128)(2,1)}, u32[]{:S(2)}, u32[]{:S(2)}) collective-permute-start(bf16[4,128,128]{2,1,0:T(8,128)(2,1)} %fusion.4), channel_id=1, source_target_pairs={{24,0},{26,2},{28,4},{30,6},{25,1},{27,3},{29,5},{31,7}} | collective-permute-start | bytes 393224 | tf_op jit(solution)/shard_map/ppermute | solution.py:393
  209.5 1.2 copy-start.2
  210.8 1.2 copy-start.6
  212.0 1.6 copy-start.12
  213.6 1.0 copy-start.14
  214.6 1.2 copy-start.22
  226.0 1.3 copy-start.7
  227.3 1.4 copy-start.9
  228.7 5.4 %copy-start.30 = (f32[4]{0:T(128)S(1)}, f32[4]{0:T(128)}, u32[]{:S(2)}) copy-start(f32[4]{0:T(128)} %get-tuple-element.59) | copy-start | bytes 52
  228.7 5.4 %copy-start.31 = (f32[4]{0:T(128)S(1)}, f32[4]{0:T(128)}, u32[]{:S(2)}) copy-start(f32[4]{0:T(128)} %get-tuple-element.60) | copy-start | bytes 52
  229.7 11.8 %copy-start.10 = (f32[256,2048]{1,0:T(8,128)S(1)}, f32[256,2048]{1,0:T(8,128)}, u32[]{:S(2)}) copy-start(f32[256,2048]{1,0:T(8,128)} %copy-done.9) | copy-start | bytes 6291460
  231.2 10.2 %collective-permute-start.8 = (bf16[4,128,128]{2,1,0:T(8,128)(2,1)S(1)}, bf16[4,128,128]{2,1,0:T(8,128)(2,1)S(1)}, u32[]{:S(2)}, u32[]{:S(2)}) collective-permute-start(bf16[4,128,128]{2,1,0:T(8,128)(2,1)S(1)} %fusion.24), channel_id=1, source_target_pairs={{0,6},{2,0},{4,2},{6,4},{8,14},{10,8},{12,10},{14,12},{16,22},{18,... | collective-permute-start | bytes 393224 | tf_op jit(solution)/shard_map/ppermute | solution.py:354
  231.3 10.2 %copy-start.3 = (bf16[256,2048]{1,0:T(8,128)(2,1)S(1)}, bf16[256,2048]{1,0:T(8,128)(2,1)}, u32[]{:S(2)}) copy-start(bf16[256,2048]{1,0:T(8,128)(2,1)} %v.7) | copy-start | bytes 3145732
  231.3 10.2 %copy-start.8 = (f32[256,2048]{1,0:T(8,128)S(1)}, f32[256,2048]{1,0:T(8,128)}, u32[]{:S(2)}) copy-start(f32[256,2048]{1,0:T(8,128)} %copy-done.7) | copy-start | bytes 6291460
  232.9 8.5 %collective-permute-start.7 = (bf16[4,128,128]{2,1,0:T(8,128)(2,1)S(1)}, bf16[4,128,128]{2,1,0:T(8,128)(2,1)S(1)}, u32[]{:S(2)}, u32[]{:S(2)}) collective-permute-start(bf16[4,128,128]{2,1,0:T(8,128)(2,1)S(1)} %fusion.19), channel_id=1, source_target_pairs={{0,4},{2,6},{4,0},{6,2},{8,12},{10,14},{12,8},{14,10},{16,20},{18,... | collective-permute-start | bytes 393224 | tf_op jit(solution)/shard_map/ppermute | solution.py:354
  235.4 5.9 %collective-permute-start.6 = (bf16[4,128,128]{2,1,0:T(8,128)(2,1)S(1)}, bf16[4,128,128]{2,1,0:T(8,128)(2,1)S(1)}, u32[]{:S(2)}, u32[]{:S(2)}) collective-permute-start(bf16[4,128,128]{2,1,0:T(8,128)(2,1)S(1)} %fusion.14), channel_id=1, source_target_pairs={{0,2},{2,4},{4,6},{6,0},{8,10},{10,12},{12,14},{14,8},{16,18},{18,... | collective-permute-start | bytes 393224 | tf_op jit(solution)/shard_map/ppermute | solution.py:354
  241.5 7.6 %copy-start.26 = (bf16[256,4096]{1,0:T(8,128)(2,1)S(1)}, bf16[256,4096]{1,0:T(8,128)(2,1)}, u32[]{:S(2)}) copy-start(bf16[256,4096]{1,0:T(8,128)(2,1)} %get-tuple-element.86) | copy-start | bytes 6291460
  249.1 1.3 copy-start.29
  249.1 2.0 copy-start.28
